TPU v7x, 32 devices: a whole 2x2x4 slice. The times are simulated.
32 devices in a mesh: groups: 2 (over y), gx: 4 (over x, core), gy: 4 (over z).
Axes of the slice: x: 2, y: 2, z: 4, core: 2. Of those that a mesh axis runs over, the one named last changes fastest.
Arguments:
- layer_input: bfloat16 [384, 16384], P(('groups', 'gx'), 'gy'), parts along dimension 0, may hold values from -0.4375 to 0.4375
- packed_weight: bfloat16 [16384, 10240], P('gy', 'gx'), may hold values from -0.046875 to 0.046875
- packed_cotangent: bfloat16 [384, 10240], P(('groups', 'gy'), 'gx'), parts along dimension 0, may hold values from -8 to 8
- context: bfloat16 [384, 8192], P(('groups', 'gx'), 'gy'), parts along dimension 0, may hold values from -0.4375 to 0.4375
- mixing_weight: bfloat16 [8192, 16384], P('gy', 'gx'), may hold values from -0.0625 to 0.0625
- mixing_cotangent: bfloat16 [384, 16384], P(('groups', 'gy'), 'gx'), parts along dimension 0, may hold values from -8 to 8
Outputs:
- input_gradient: bfloat16 [384, 16384], P(('groups', 'gx'), 'gy'), parts along dimension 0
- packed_gradient: bfloat16 [32768, 10240], P(('groups', 'gy'), 'gx'), parts along dimension 0
- context_gradient: bfloat16 [384, 8192], P(('groups', 'gx'), 'gy'), parts along dimension 0
- mixing_gradient: bfloat16 [16384, 16384], P(('groups', 'gy'), 'gx'), parts along dimension 0
There are 2 independent parts, one for each index of `groups`. A program takes and returns all parts, laid end to end along the dimension named above; an argument that names none is the same for every part. Nothing has to cross between parts.
All inputs are finite; a program needn't handle non-finite values.
Results may differ from a plain program's by a relative error of at most 0.009.
Values may be sent and summed in bfloat16 or wider, within the bound.
A program may use at most 192 MiB of HBM per device.

v0:
```python
import jax
import jax.numpy as jnp
from jax import lax
from jax.sharding import PartitionSpec as P


def transposed_product(left, right):
    return lax.dot_general(
        left, right, (((0,), (0,)), ((), ())), preferred_element_type=jnp.float32
    )


def weight_product(cotangent_rows, weight):
    return lax.dot_general(
        cotangent_rows, weight, (((1,), (1,)), ((), ())), preferred_element_type=jnp.float32
    )


def accumulate(cotangent_rows, portion):
    return transposed_product(portion, cotangent_rows)


def block_product(cotangent_rows, weight):
    return weight_product(cotangent_rows, weight)


def body(layer_input, packed_weight, packed_cotangent, context, mixing_weight, mixing_cotangent):
    packed_rows = lax.all_gather(packed_cotangent, "gy", axis=0, tiled=True)
    packed_total = accumulate(packed_rows, lax.all_gather(layer_input, "gx", axis=0, tiled=True))
    mixing_rows = lax.all_gather(mixing_cotangent, "gy", axis=0, tiled=True)
    mixing_total = accumulate(mixing_rows, lax.all_gather(context, "gx", axis=0, tiled=True))
    input_summed = lax.psum_scatter(
        block_product(packed_rows, packed_weight).astype(jnp.bfloat16),
        "gx",
        scatter_dimension=0,
        tiled=True,
    )
    context_summed = lax.psum_scatter(
        block_product(mixing_rows, mixing_weight).astype(jnp.bfloat16),
        "gx",
        scatter_dimension=0,
        tiled=True,
    )
    return (
        input_summed,
        packed_total.astype(jnp.bfloat16),
        context_summed,
        mixing_total.astype(jnp.bfloat16),
    )


def solution(mesh):
    return jax.shard_map(
        body,
        mesh=mesh,
        in_specs=(
            P(("groups", "gx"), "gy"),
            P("gy", "gx"),
            P(("groups", "gy"), "gx"),
            P(("groups", "gx"), "gy"),
            P("gy", "gx"),
            P(("groups", "gy"), "gx"),
        ),
        out_specs=(
            P(("groups", "gx"), "gy"),
            P(("groups", "gy"), "gx"),
            P(("groups", "gx"), "gy"),
            P(("groups", "gy"), "gx"),
        ),
        check_vma=False,
    )
```

profile of v0, /device:TPU:0, one launch (start us, length us, event | category | flops | bytes accessed | tf_op | source)
XLA Modules:
  0.0 141.9 jit_solution(14101914765180916408)
XLA Ops:
  7.2 0.0 all-gather.5.cloned.1.call-start
  7.2 0.7 all-gather.5.cloned.1.call-update
  7.9 0.0 all-gather.3.cloned.1.call-start
  7.9 0.7 all-gather.3.cloned.1.call-update
  8.6 0.0 reduce-scatter.3.cloned.1.call-start
  8.7 32.6 %all_gather.12 = bf16[192,2560]{1,0:T(8,128)(2,1)S(1)} all-gather(bf16[48,2560]{1,0:T(8,128)(2,1)} %param.8), channel_id=1, replica_groups=mesh['groups'=2,'gx'=4,'gy'=4] {'gy'}, dimensions={0}, use_global_device_ids=true | all-gather | bytes 1228800 | tf_op jit(solution)/shard_map/all_gather | solution.py:28
  41.3 0.0 copy-start.1
  41.3 12.5 %convolution_convert_fusion.2 = bf16[192,4096]{1,0:T(8,128)(2,1)} fusion(bf16[192,2560]{1,0:T(8,128)(2,1)S(1)} %all_gather.12, bf16[4096,2560]{1,0:T(8,128)(2,1)} %param.7), kind=kOutput, calls=%fused_computation.2 | convolution fusion | flops 4027318272 | bytes 23527424 | tf_op jit(solution)/shard_map/dot_general | solution.py:14
  53.8 0.0 reduce-scatter.3.cloned.1.call-update
  53.8 0.0 reduce-scatter.5.cloned.1.call-start
  53.8 0.0 copy-done.1
  53.8 8.6 %all_gather.15 = bf16[192,2048]{1,0:T(8,128)(2,1)S(1)} all-gather(bf16[48,2048]{1,0:T(8,128)(2,1)S(1)} %copy-done.1), channel_id=1, replica_groups=mesh['groups'=2,'gx'=4,'gy'=4] {'gx'}, dimensions={0}, use_global_device_ids=true | all-gather | bytes 983040 | tf_op jit(solution)/shard_map/all_gather | solution.py:31
  62.4 0.0 all-gather.5.cloned.1.call-done
  62.4 0.0 copy-start
  62.4 13.5 %convolution_convert_fusion.3 = bf16[192,2048]{1,0:T(8,128)(2,1)} fusion(bf16[192,4096]{1,0:T(8,128)(2,1)} %all-gather.5.cloned.1.call-done, bf16[2048,4096]{1,0:T(8,128)(2,1)} %param.10), kind=kOutput, calls=%fused_computation.3 | convolution fusion | flops 3221618688 | bytes 19136512 | tf_op jit(solution)/shard_map/dot_general | solution.py:14
  75.9 0.0 reduce-scatter.5.cloned.1.call-update
  75.9 0.0 copy-done
  75.9 8.6 %convolution_convert_fusion.1 = bf16[2048,4096]{1,0:T(8,128)(2,1)} fusion(bf16[192,2048]{1,0:T(8,128)(2,1)S(1)} %all_gather.15, bf16[192,4096]{1,0:T(8,128)(2,1)S(1)} %copy-done), kind=kOutput, calls=%fused_computation.1 | convolution fusion | flops 3229614080 | bytes 19136512 | tf_op jit(solution)/shard_map/dot_general | solution.py:8
  84.5 0.0 all-gather.3.cloned.1.call-done
  84.5 11.9 %convolution_convert_fusion = bf16[4096,2560]{1,0:T(8,128)(2,1)} fusion(bf16[192,4096]{1,0:T(8,128)(2,1)} %all-gather.3.cloned.1.call-done, bf16[192,2560]{1,0:T(8,128)(2,1)S(1)} %all_gather.12), kind=kOutput, calls=%fused_computation | convolution fusion | flops 4037017600 | bytes 23527424 | tf_op jit(solution)/shard_map/dot_general | solution.py:8
  96.4 12.5 %reduce-scatter.3.cloned.1.call-done = bf16[48,4096]{1,0:T(8,128)(2,1)} async-done(((bf16[192,4096]{1,0:T(8,128)(2,1)}), bf16[48,4096]{1,0:T(8,128)(2,1)}) %reduce-scatter.3.cloned.1.call-update) | async-done | bytes 393232 | tf_op jit(solution)/shard_map/reduce_scatter | solution.py:32
  108.9 26.4 %reduce-scatter.5.cloned.1.call-done = bf16[48,2048]{1,0:T(8,128)(2,1)} async-done(((bf16[192,2048]{1,0:T(8,128)(2,1)}), bf16[48,2048]{1,0:T(8,128)(2,1)}) %reduce-scatter.5.cloned.1.call-update) | async-done | bytes 196624 | tf_op jit(solution)/shard_map/reduce_scatter | solution.py:38
Async XLA Ops:
  7.2 55.2 %all-gather.5.cloned.1.call-start = ((), (), s32[]{:S(2)}) async-start(), calls=%async_computation.4 | async-start | bytes 1966080 | tf_op jit(solution)/shard_map/all_gather | solution.py:30
  7.9 76.6 %all-gather.3.cloned.1.call-start = ((), (), s32[]{:S(2)}) async-start(), calls=%async_computation.3 | async-start | bytes 1966080 | tf_op jit(solution)/shard_map/all_gather | solution.py:29
  8.6 100.3 %reduce-scatter.3.cloned.1.call-start = ((), (), s32[]{:S(2)}) async-start(), calls=%async_computation.2 | async-start | bytes 1966080 | tf_op jit(solution)/shard_map/reduce_scatter | solution.py:32
  41.3 12.6 %copy-start.1 = (bf16[48,2048]{1,0:T(8,128)(2,1)S(1)}, bf16[48,2048]{1,0:T(8,128)(2,1)}, u32[]{:S(2)}) copy-start(bf16[48,2048]{1,0:T(8,128)(2,1)} %param.9) | copy-start | bytes 589828
  53.8 81.6 %reduce-scatter.5.cloned.1.call-start = ((), (), s32[]{:S(2)}) async-start(), calls=%async_computation.5 | async-start | bytes 983040 | tf_op jit(solution)/shard_map/reduce_scatter | solution.py:38
  62.4 13.5 %copy-start = (bf16[192,4096]{1,0:T(8,128)(2,1)S(1)}, bf16[192,4096]{1,0:T(8,128)(2,1)}, u32[]{:S(2)}) copy-start(bf16[192,4096]{1,0:T(8,128)(2,1)} %all-gather.5.cloned.1.call-done) | copy-start | bytes 4718596
Sparse Core Ops, SparseCore 0:
  9.6 47.4 all-gather.4
  58.6 18.9 all-gather.2
  80.8 28.1 reduce-scatter.2
  112.1 23.2 reduce-scatter.4
where the time goes:
time: 142 us
  matrix products  46.4 us (33%)
  blocking collectives  41.1 us (29%)
  waiting for transfers between devices  40.4 us (28%)
  between operations  13.8 us (10%)
    all_gather x1, blocking collectives, body(): packed_rows = lax.all_gather(packed_cotangent, 'gy', axis=0, tiled=True)  32.6 us
    reduce_scatter x1, waiting for transfers between devices, body(): lax.psum_scatter(block_product(mixing_rows, mixing_weight).astype(jnp.bfl...  26.4 us
    dot_general x2, matrix products, weight_product(): lax.dot_general(cotangent_rows, weight, (((1,), (1,)), ((), ())), preferr...  26 us
    dot_general x2, matrix products, transposed_product(): lax.dot_general(left, right, (((0,), (0,)), ((), ())), preferred_element_...  20.5 us
    reduce_scatter x1, waiting for transfers between devices, body(): lax.psum_scatter(block_product(packed_rows, packed_weight).astype(jnp.bfl...  12.5 us
    all_gather x1, blocking collectives, body(): lax.all_gather(context, 'gx', axis=0, tiled=True)  8.57 us
  transfers between devices with their start and end apart: 4, of which 2 were waited for; matrix products, arithmetic and copies ran while one was open for 33% of the time, Pallas kernels for 0%

commit v1 on v0

v1 whole, which is shorter than its diff:
```python
import functools

import jax
import jax.numpy as jnp
from jax import lax
from jax.experimental import pallas as pl
from jax.experimental.pallas import tpu as pltpu
from jax.sharding import PartitionSpec as P

BF16 = jnp.bfloat16
F32 = jnp.float32
MESH = pl.DeviceIdType.MESH
ANY = pl.ANY
AHEAD = 3


def exchange_kernel(
    n_gx, n_gy, g_chunks, h_chunks,
    x_in, w_in, g_in, c_in, m_in, h_in,
    xt_out, ct_out, gall_out, hall_out, dx_out, dc_out,
    wv, mv, gall, hall, xall, call, xt, ct, acc_x, acc_c,
    term_x, part_x, pair_x, cross_x, res_x,
    term_c, part_c, pair_c, cross_c, res_c,
    w_sem, m_sem, own_sem, g_send, g_recv, h_send, h_recv,
    xs_send, xs_recv, cs_send, cs_recv,
    px_send, px_recv, cx_send, cx_recv, pc_send, pc_recv, cc_send, cc_recv,
    out_sem,
):
    gx = lax.axis_index("gx")
    z = lax.axis_index("gy")
    core = lax.rem(gx, 2)
    chip = gx // 2
    partner = gx + 1 - 2 * core
    n_chips = n_gx // 2
    g_width = g_in.shape[1] // g_chunks
    h_width = h_in.shape[1] // h_chunks
    rows = g_in.shape[0]
    tokens = rows * n_gy

    def peer(s):
        return 2 * lax.rem(chip + s, n_chips) + core

    loads_w = [
        pltpu.make_async_copy(w_in.at[:, pl.ds(c * g_width, g_width)], wv.at[c], w_sem.at[c])
        for c in range(g_chunks)
    ]
    loads_m = [
        pltpu.make_async_copy(m_in.at[:, pl.ds(c * h_width, h_width)], mv.at[c], m_sem.at[c])
        for c in range(h_chunks)
    ]
    own = [
        pltpu.make_async_copy(g_in, gall.at[z], own_sem.at[0]),
        pltpu.make_async_copy(h_in, hall.at[z], own_sem.at[1]),
        pltpu.make_async_copy(x_in, xall.at[gx], own_sem.at[2]),
        pltpu.make_async_copy(c_in, call.at[gx], own_sem.at[3]),
    ]
    for copy in own:
        copy.start()
    for copy in loads_w:
        copy.start()
    for copy in loads_m:
        copy.start()

    barrier = pltpu.get_barrier_semaphore()

    def greet(**where):
        pl.semaphore_signal(barrier, inc=1, device_id=where, device_id_type=MESH)

    greet(gx=partner)
    for s in range(1, n_chips):
        greet(gx=peer(s))

    @pl.when(z > 0)
    def _():
        greet(gy=z - 1)

    @pl.when(z < n_gy - 1)
    def _():
        greet(gy=z + 1)

    ends = jnp.where(z > 0, 1, 0) + jnp.where(z < n_gy - 1, 1, 0)
    pl.semaphore_wait(barrier, n_chips + ends)

    chunks = [("g", c) for c in range(g_chunks)] + [("h", c) for c in range(h_chunks)]

    def chain_copy(kind, c, way, block, source=None):
        if kind == "g":
            buf, send, recv, width = gall, g_send, g_recv, g_width
        else:
            buf, send, recv, width = hall, h_send, h_recv, h_width
        columns = pl.ds(c * width, width)
        src = buf.at[block, :, columns] if source is None else source.at[:, columns]
        return pltpu.make_async_remote_copy(
            src_ref=src,
            dst_ref=buf.at[block, :, columns],
            send_sem=send.at[way, block, c],
            recv_sem=recv.at[block, c],
            device_id={"gy": z + 1 if way == 0 else z - 1},
            device_id_type=MESH,
        )

    def send_own(index):
        kind, c = chunks[index]
        source = g_in if kind == "g" else h_in

        @pl.when(z < n_gy - 1)
        def _():
            chain_copy(kind, c, 0, z, source).start()

        @pl.when(z > 0)
        def _():
            chain_copy(kind, c, 1, z, source).start()

    def forward(index):
        kind, c = chunks[index]
        for s in range(1, n_gy):
            @pl.when(z - s >= 0)
            def _():
                copy = chain_copy(kind, c, 0, z - s)
                copy.wait_recv()

                @pl.when(z < n_gy - 1)
                def _():
                    copy.start()

            @pl.when(z + s <= n_gy - 1)
            def _():
                copy = chain_copy(kind, c, 1, z + s)
                copy.wait_recv()

                @pl.when(z > 0)
                def _():
                    copy.start()

    def drain(index):
        kind, c = chunks[index]
        for s in range(n_gy):
            @pl.when((z - s >= 0) & (z < n_gy - 1))
            def _():
                chain_copy(kind, c, 0, z - s).wait_send()

            @pl.when((z + s <= n_gy - 1) & (z > 0))
            def _():
                chain_copy(kind, c, 1, z + s).wait_send()

    def cross_gather(s, source, buf, send, recv, arrived=False):
        slot = 2 * lax.rem(chip - s + n_chips, n_chips) + core if arrived else gx
        return pltpu.make_async_remote_copy(
            src_ref=source, dst_ref=buf.at[slot], send_sem=send.at[s - 1], recv_sem=recv.at[s - 1],
            device_id={"gx": peer(s)}, device_id_type=MESH,
        )

    def core_gather(s, source, buf, send, recv):
        slot = 2 * lax.rem(chip - s + n_chips, n_chips) + core
        index = n_chips - 1 + s
        return pltpu.make_async_remote_copy(
            src_ref=buf.at[slot] if source is None else source,
            dst_ref=buf.at[slot], send_sem=send.at[index], recv_sem=recv.at[index],
            device_id={"gx": partner}, device_id_type=MESH,
        )

    def start_gather(source, buf, send, recv):
        for s in range(1, n_chips):
            cross_gather(s, source, buf, send, recv).start()
        core_gather(0, source, buf, send, recv).start()

    def pass_gather(source, buf, send, recv):
        for s in range(1, n_chips):
            cross_gather(s, source, buf, send, recv, True).wait_recv()
            core_gather(s, None, buf, send, recv).start()

    def end_gather(source, buf, send, recv):
        core_gather(0, source, buf, send, recv).wait()
        for s in range(1, n_chips):
            cross_gather(s, source, buf, send, recv).wait_send()
            core_gather(s, None, buf, send, recv).wait()

    def transpose_into(buf, out, pieces):
        width = buf.shape[2] // pieces

        @pl.loop(0, pieces)
        def _(i):
            columns = pl.ds(pl.multiple_of(i * width, width), width)
            block = buf[:, :, columns].reshape(tokens, width)
            out[columns, :] = block.T

    def multiply(index):
        kind, c = chunks[index]
        if kind == "g":
            buf, weight, load, acc, width = gall, wv, loads_w, acc_x, g_width
        else:
            buf, weight, load, acc, width = hall, mv, loads_m, acc_c, h_width
        load[c].wait()
        outs = acc.shape[1]
        tile = min(512, outs // 2)
        left = buf[:, :, c * width:(c + 1) * width].reshape(tokens, width)

        @pl.loop(0, outs // tile)
        def _(i):
            at = pl.ds(pl.multiple_of(i * tile, tile), tile)
            product = lax.dot_general(
                left, weight[c, at, :], (((1,), (1,)), ((), ())), preferred_element_type=F32
            )
            if c == 0:
                acc[:, at] = product
            else:
                acc[:, at] += product

    def to_partner(k, term, part, send, recv):
        return pltpu.make_async_remote_copy(
            src_ref=term.at[2 * k + 1 - core], dst_ref=part.at[k],
            send_sem=send.at[k], recv_sem=recv.at[k],
            device_id={"gx": partner}, device_id_type=MESH,
        )

    def to_chip(s, pair, cross, send, recv):
        return pltpu.make_async_remote_copy(
            src_ref=pair.at[s - 1], dst_ref=cross.at[s - 1],
            send_sem=send.at[s - 1], recv_sem=recv.at[s - 1],
            device_id={"gx": peer(s)}, device_id_type=MESH,
        )

    def scatter_first(acc, term, part, send, recv):
        size = acc.shape[0] // n_gx
        for b in range(n_gx):
            term[b] = acc[b * size:(b + 1) * size, :].astype(BF16)
        for k in range(n_chips):
            to_partner(k, term, part, send, recv).start()

    def scatter_second(term, part, send, recv, pair, cross, send2, recv2):
        for k in range(n_chips):
            to_partner(k, term, part, send, recv).wait()
        for s in range(1, n_chips):
            k = lax.rem(chip + s, n_chips)
            pair[s - 1] = (term[2 * k + core].astype(F32) + part[k].astype(F32)).astype(BF16)
            to_chip(s, pair, cross, send2, recv2).start()

    def scatter_last(term, part, pair, cross, send2, recv2, res):
        for s in range(1, n_chips):
            to_chip(s, pair, cross, send2, recv2).wait()
        total = term[gx].astype(F32) + part[chip].astype(F32)
        for s in range(1, n_chips):
            total = total + cross[s - 1].astype(F32)
        res[...] = total.astype(BF16)

    outs = [
        pltpu.make_async_copy(gall, gall_out, out_sem.at[0]),
        pltpu.make_async_copy(hall, hall_out, out_sem.at[1]),
        pltpu.make_async_copy(xt, xt_out, out_sem.at[2]),
        pltpu.make_async_copy(ct, ct_out, out_sem.at[3]),
        pltpu.make_async_copy(res_x, dx_out, out_sem.at[4]),
        pltpu.make_async_copy(res_c, dc_out, out_sem.at[5]),
    ]
    x_gather = (x_in, xall, xs_send, xs_recv)
    c_gather = (c_in, call, cs_send, cs_recv)

    for index in range(AHEAD):
        send_own(index)
    start_gather(*x_gather)
    start_gather(*c_gather)
    for copy in own:
        copy.wait()
    for index in range(len(chunks)):
        forward(index)
        if index + AHEAD < len(chunks):
            send_own(index + AHEAD)
        multiply(index)
        after = index - g_chunks + 1
        if after == -1:
            pass_gather(*x_gather)
            pass_gather(*c_gather)
        if after == 0:
            outs[0].start()
            scatter_first(acc_x, term_x, part_x, px_send, px_recv)
            end_gather(*x_gather)
            transpose_into(xall, xt, 8)
            outs[2].start()
        if after == 1:
            scatter_second(term_x, part_x, px_send, px_recv, pair_x, cross_x, cx_send, cx_recv)
            end_gather(*c_gather)
            transpose_into(call, ct, 4)
            outs[3].start()
    outs[1].start()
    scatter_first(acc_c, term_c, part_c, pc_send, pc_recv)
    scatter_last(term_x, part_x, pair_x, cross_x, cx_send, cx_recv, res_x)
    outs[4].start()
    scatter_second(term_c, part_c, pc_send, pc_recv, pair_c, cross_c, cc_send, cc_recv)
    for index in range(len(chunks)):
        drain(index)
    scatter_last(term_c, part_c, pair_c, cross_c, cc_send, cc_recv, res_c)
    outs[5].start()
    for copy in outs:
        copy.wait()


def exchange(n_gx, n_gy, x, w, g, c, m, h):
    g_chunks, h_chunks = 5, 4
    rows_g, rows_x = g.shape[0], x.shape[0]
    d, fp, ck, fm = x.shape[1], g.shape[1], c.shape[1], h.shape[1]
    tokens = rows_g * n_gy
    nc = n_gx // 2
    more = max(nc - 1, 1)
    dma = pltpu.SemaphoreType.DMA
    vm = pltpu.VMEM

    def scatter(width):
        return [
            vm((n_gx, rows_x, width), BF16), vm((nc, rows_x, width), BF16),
            vm((more, rows_x, width), BF16), vm((more, rows_x, width), BF16),
            vm((rows_x, width), BF16),
        ]

    shape = jax.ShapeDtypeStruct
    flops = 2 * tokens * (d * fp + ck * fm)
    return pl.pallas_call(
        functools.partial(exchange_kernel, n_gx, n_gy, g_chunks, h_chunks),
        out_shape=(
            shape((d, tokens), BF16), shape((ck, tokens), BF16),
            shape((n_gy, rows_g, fp), BF16), shape((n_gy, rows_g, fm), BF16),
            shape((rows_x, d), BF16), shape((rows_x, ck), BF16),
        ),
        in_specs=[pl.BlockSpec(memory_space=ANY)] * 6,
        out_specs=[pl.BlockSpec(memory_space=ANY)] * 6,
        scratch_shapes=[
            vm((g_chunks, d, fp // g_chunks), BF16), vm((h_chunks, ck, fm // h_chunks), BF16),
            vm((n_gy, rows_g, fp), BF16), vm((n_gy, rows_g, fm), BF16),
            vm((n_gx, rows_x, d), BF16), vm((n_gx, rows_x, ck), BF16),
            vm((d, tokens), BF16), vm((ck, tokens), BF16),
            vm((tokens, d), F32), vm((tokens, ck), F32),
            *scatter(d), *scatter(ck),
            dma((g_chunks,)), dma((h_chunks,)), dma((4,)),
            dma((2, n_gy, g_chunks)), dma((n_gy, g_chunks)),
            dma((2, n_gy, h_chunks)), dma((n_gy, h_chunks)),
            dma((2 * nc - 1,)), dma((2 * nc - 1,)), dma((2 * nc - 1,)), dma((2 * nc - 1,)),
            dma((nc,)), dma((nc,)), dma((more,)), dma((more,)),
            dma((nc,)), dma((nc,)), dma((more,)), dma((more,)),
            dma((6,)),
        ],
        compiler_params=pltpu.CompilerParams(
            collective_id=0, has_side_effects=True, vmem_limit_bytes=61 * 1024 * 1024
        ),
        cost_estimate=pl.CostEstimate(flops=flops, bytes_accessed=2 * (d * fp + ck * fm), transcendentals=0),
        name="exchange",
    )(x, w, g, c, m, h)


SLOTS = 3


def gradients_kernel(g_steps, h_steps, xt, ct, gall, hall, dw, dm, xv, cv, gv, hv, wbuf, mbuf, in_sem, w_sem, m_sem):
    first = [
        pltpu.make_async_copy(gall, gv, in_sem.at[0]),
        pltpu.make_async_copy(xt, xv, in_sem.at[1]),
        pltpu.make_async_copy(hall, hv, in_sem.at[2]),
        pltpu.make_async_copy(ct, cv, in_sem.at[3]),
    ]
    for copy in first:
        copy.start()

    def run(steps, pieces, left, right, buf, sem, out):
        tall = out.shape[0] // steps
        wide = out.shape[1] // pieces

        def copy_out(i, slot):
            at = pl.ds(pl.multiple_of(i * tall, tall), tall)
            return pltpu.make_async_copy(buf.at[slot], out.at[at, :], sem.at[slot])

        @pl.loop(0, steps)
        def _(i):
            slot = lax.rem(i, SLOTS)

            @pl.when(i >= SLOTS)
            def _():
                copy_out(i - SLOTS, slot).wait()

            part = left[pl.ds(pl.multiple_of(i * tall, tall), tall), :]
            for p in range(pieces):
                columns = slice(p * wide, (p + 1) * wide)
                buf[slot, :, columns] = jnp.dot(
                    part, right[:, columns], preferred_element_type=F32
                ).astype(BF16)
            copy_out(i, slot).start()

        return [copy_out(i, i % SLOTS) for i in range(max(steps - SLOTS, 0), steps)]

    first[0].wait()
    first[1].wait()
    last = run(g_steps, 5, xv, gv, wbuf, w_sem, dw)
    first[2].wait()
    first[3].wait()
    last += run(h_steps, 4, cv, hv, mbuf, m_sem, dm)
    for copy in last:
        copy.wait()


def gradients(xt, ct, gall, hall):
    g_steps, h_steps = 8, 4
    d, tokens = xt.shape
    ck = ct.shape[0]
    fp, fm = gall.shape[1], hall.shape[1]
    dma = pltpu.SemaphoreType.DMA
    vm = pltpu.VMEM
    shape = jax.ShapeDtypeStruct
    return pl.pallas_call(
        functools.partial(gradients_kernel, g_steps, h_steps),
        out_shape=(shape((d, fp), BF16), shape((ck, fm), BF16)),
        in_specs=[pl.BlockSpec(memory_space=ANY)] * 4,
        out_specs=[pl.BlockSpec(memory_space=ANY)] * 2,
        scratch_shapes=[
            vm((d, tokens), BF16), vm((ck, tokens), BF16), vm((tokens, fp), BF16), vm((tokens, fm), BF16),
            vm((SLOTS, d // g_steps, fp), BF16), vm((SLOTS, ck // h_steps, fm), BF16),
            dma((4,)), dma((SLOTS,)), dma((SLOTS,)),
        ],
        compiler_params=pltpu.CompilerParams(vmem_limit_bytes=60 * 1024 * 1024),
        cost_estimate=pl.CostEstimate(
            flops=2 * tokens * (d * fp + ck * fm), bytes_accessed=2 * (d * fp + ck * fm), transcendentals=0
        ),
        name="gradients",
    )(xt, ct, gall, hall)


def body(n_gx, n_gy, layer_input, packed_weight, packed_cotangent, context, mixing_weight, mixing_cotangent):
    xt, ct, gall, hall, dx, dc = exchange(
        n_gx, n_gy, layer_input, packed_weight, packed_cotangent, context, mixing_weight, mixing_cotangent
    )
    tokens = xt.shape[1]
    dw, dm = gradients(xt, ct, gall.reshape(tokens, -1), hall.reshape(tokens, -1))
    return dx, dw, dc, dm


def solution(mesh):
    return jax.shard_map(
        functools.partial(body, mesh.shape["gx"], mesh.shape["gy"]),
        mesh=mesh,
        in_specs=(
            P(("groups", "gx"), "gy"),
            P("gy", "gx"),
            P(("groups", "gy"), "gx"),
            P(("groups", "gx"), "gy"),
            P("gy", "gx"),
            P(("groups", "gy"), "gx"),
        ),
        out_specs=(
            P(("groups", "gx"), "gy"),
            P(("groups", "gy"), "gx"),
            P(("groups", "gx"), "gy"),
            P(("groups", "gy"), "gx"),
        ),
        check_vma=False,
    )
```

time: 142 us -> 100 us (0.70)
  Pallas kernels: 0 us -> 97.9 us
  matrix products: 46.4 us -> 0 us
  blocking collectives: 41.1 us -> 0 us
  waiting for transfers between devices: 40.4 us -> 0 us
  between operations: 13.8 us -> 0.67 us
  local copies, waits for them, and re-layouts: 0.01 us -> 1.43 us
    pallas_call x0 -> x2, Pallas kernels: none -> 97.9 us  [the longest x1 82.1 us: exchange(): pl.pallas_call(functools.partial(exchange_kernel, n_gx, n_gy, g_chunks, h...]
    dot_general x4 -> x0, matrix products: 46.4 us -> none  [the longest x2 26 us: weight_product(): lax.dot_general(cotangent_rows, weight, (((1,), (1,)), ((), ())), preferr...]
    all_gather x2 -> x0, blocking collectives: 41.1 us -> none  [the longest x1 32.6 us: body(): packed_rows = lax.all_gather(packed_cotangent, 'gy', axis=0, tiled=True)]
    reduce_scatter x2 -> x0, waiting for transfers between devices: 39 us -> none  [the longest x1 26.4 us: body(): lax.psum_scatter(block_product(mixing_rows, mixing_weight).astype(jnp.bfl...]
    unnamed x4 -> x6, local copies, waits for them, and re-layouts: 0.01 us -> 1.43 us
  transfers between devices with their start and end apart: 4 -> 0, of which waited for: 2 -> 0; matrix products, arithmetic and copies ran while one was open for 33% -> 0% of each run, Pallas kernels for 0% -> 0%
where the time goes in v1:
time: 100 us
  Pallas kernels  97.9 us (98%)
  local copies, waits for them, and re-layouts  1.43 us (1%)
    pallas_call x1, Pallas kernels, exchange(): pl.pallas_call(functools.partial(exchange_kernel, n_gx, n_gy, g_chunks, h...  82.1 us
    pallas_call x1, Pallas kernels, gradients(): pl.pallas_call(functools.partial(gradients_kernel, g_steps, h_steps), out...  15.8 us

profile of v1, /device:TPU:0, one launch (start us, length us, event | category | flops | bytes accessed | tf_op | source)
XLA Modules:
  0.0 100.0 jit_solution(11915609065930179197)
XLA Ops:
  0.6 82.1 %exchange.1 = (bf16[4096,192]{1,0:T(8,128)(2,1)}, bf16[2048,192]{1,0:T(8,128)(2,1)}, bf16[4,48,2560]{2,1,0:T(8,128)(2,1)}, bf16[4,48,4096]{2,1,0:T(8,128)(2,1)},...) custom-call(bf16[48,4096]{1,0:T(8,128)(2,1)} %x_in.1, bf16[4096,2560]{1,0:T(8,128)(2,1)} %w_in.1, ...), custom_call_target="tpu_custom_call" | custom-call | flops 7247757312 | bytes 37748736 | tf_op jit(solution)/shard_map/exchange/pallas_call | solution.py:315
  82.8 0.0 copy-start
  82.8 0.0 copy-start.1
  82.8 15.8 %gradients.1 = (bf16[4096,2560]{1,0:T(8,128)(2,1)}, bf16[2048,4096]{1,0:T(8,128)(2,1)}) custom-call(bf16[4096,192]{1,0:T(8,128)(2,1)} %get-tuple-element.13.xt, bf16[2048,192]{1,0:T(8,128)(2,1)} %get-tuple-element.14.ct, bf16[192,2560]{1,0:T(8,128)(2,1)} %bitcast.3, bf16[192,4096]{1,0:T(8,128)(2,1)} %bitcast.2), custom_call_target="tpu_custom_call" | custom-call | flops 7247757312 | bytes 37748736 | tf_op jit(solution)/shard_map/gradients/pallas_call | solution.py:404
  98.6 0.0 copy-done
  98.6 0.7 copy.12
  99.4 0.0 copy-done.1
  99.4 0.7 copy.13
Async XLA Ops:
  82.8 15.8 %copy-start = (bf16[48,4096]{1,0:T(8,128)(2,1)S(1)}, bf16[48,4096]{1,0:T(8,128)(2,1)}, u32[]{:S(2)}) copy-start(bf16[48,4096]{1,0:T(8,128)(2,1)} %get-tuple-element.24) | copy-start | bytes 1179652
  82.8 16.6 %copy-start.1 = (bf16[48,2048]{1,0:T(8,128)(2,1)S(1)}, bf16[48,2048]{1,0:T(8,128)(2,1)}, u32[]{:S(2)}) copy-start(bf16[48,2048]{1,0:T(8,128)(2,1)} %get-tuple-element.26) | copy-start | bytes 589828

commit v2 on v1

--- a/solution.py
+++ b/solution.py
@@ -12,13 +12,14 @@
 MESH = pl.DeviceIdType.MESH
 ANY = pl.ANY
 AHEAD = 3
+TILE = 2048
 
 
 def exchange_kernel(
     n_gx, n_gy, g_chunks, h_chunks,
     x_in, w_in, g_in, c_in, m_in, h_in,
     xt_out, ct_out, gall_out, hall_out, dx_out, dc_out,
-    wv, mv, gall, hall, xall, call, xt, ct, acc_x, acc_c,
+    wv, mv, gall, hall, xall, call, xt, ct, acc_x, acc_c, flip,
     term_x, part_x, pair_x, cross_x, res_x,
     term_c, part_c, pair_c, cross_c, res_c,
     w_sem, m_sem, own_sem, g_send, g_recv, h_send, h_recv,
@@ -49,12 +50,17 @@
         for c in range(h_chunks)
     ]
     own = [
-        pltpu.make_async_copy(g_in, gall.at[z], own_sem.at[0]),
-        pltpu.make_async_copy(h_in, hall.at[z], own_sem.at[1]),
-        pltpu.make_async_copy(x_in, xall.at[gx], own_sem.at[2]),
-        pltpu.make_async_copy(c_in, call.at[gx], own_sem.at[3]),
-    ]
-    for copy in own:
+        pltpu.make_async_copy(x_in, xall.at[gx], own_sem.at[0]),
+        pltpu.make_async_copy(c_in, call.at[gx], own_sem.at[1]),
+    ]
+    own_blocks = [
+        pltpu.make_async_copy(g_in.at[:, pl.ds(c * g_width, g_width)], gall.at[c, z], own_sem.at[2 + c])
+        for c in range(g_chunks)
+    ] + [
+        pltpu.make_async_copy(h_in.at[:, pl.ds(c * h_width, h_width)], hall.at[c, z], own_sem.at[2 + g_chunks + c])
+        for c in range(h_chunks)
+    ]
+    for copy in own_blocks + own:
         copy.start()
     for copy in loads_w:
         copy.start()
@@ -70,46 +76,45 @@
     for s in range(1, n_chips):
         greet(gx=peer(s))
 
-    @pl.when(z > 0)
-    def _():
-        greet(gy=z - 1)
-
-    @pl.when(z < n_gy - 1)
-    def _():
-        greet(gy=z + 1)
-
-    ends = jnp.where(z > 0, 1, 0) + jnp.where(z < n_gy - 1, 1, 0)
+    ends = 0
+    for hops in (1, 2):
+        @pl.when(z - hops >= 0)
+        def _():
+            greet(gy=z - hops)
+
+        @pl.when(z + hops < n_gy)
+        def _():
+            greet(gy=z + hops)
+
+        ends += jnp.where(z - hops >= 0, 1, 0) + jnp.where(z + hops < n_gy, 1, 0)
+
     pl.semaphore_wait(barrier, n_chips + ends)
 
     chunks = [("g", c) for c in range(g_chunks)] + [("h", c) for c in range(h_chunks)]
 
-    def chain_copy(kind, c, way, block, source=None):
-        if kind == "g":
-            buf, send, recv, width = gall, g_send, g_recv, g_width
-        else:
-            buf, send, recv, width = hall, h_send, h_recv, h_width
-        columns = pl.ds(c * width, width)
-        src = buf.at[block, :, columns] if source is None else source.at[:, columns]
+    def chain_copy(kind, c, way, block, hops=1):
+        buf, send, recv = (gall, g_send, g_recv) if kind == "g" else (hall, h_send, h_recv)
         return pltpu.make_async_remote_copy(
-            src_ref=src,
-            dst_ref=buf.at[block, :, columns],
-            send_sem=send.at[way, block, c],
+            src_ref=buf.at[c, block],
+            dst_ref=buf.at[c, block],
+            send_sem=send.at[way + 2 * (hops - 1), block, c],
             recv_sem=recv.at[block, c],
-            device_id={"gy": z + 1 if way == 0 else z - 1},
+            device_id={"gy": z + hops if way == 0 else z - hops},
             device_id_type=MESH,
         )
 
     def send_own(index):
         kind, c = chunks[index]
-        source = g_in if kind == "g" else h_in
-
-        @pl.when(z < n_gy - 1)
-        def _():
-            chain_copy(kind, c, 0, z, source).start()
-
-        @pl.when(z > 0)
-        def _():
-            chain_copy(kind, c, 1, z, source).start()
+        own_blocks[index].wait()
+
+        for hops in (2, 1):
+            @pl.when(z + hops < n_gy)
+            def _():
+                chain_copy(kind, c, 0, z, hops).start()
+
+            @pl.when(z - hops >= 0)
+            def _():
+                chain_copy(kind, c, 1, z, hops).start()
 
     def forward(index):
         kind, c = chunks[index]
@@ -118,23 +123,32 @@
             def _():
                 copy = chain_copy(kind, c, 0, z - s)
                 copy.wait_recv()
-
-                @pl.when(z < n_gy - 1)
-                def _():
-                    copy.start()
+                if s >= 2:
+                    @pl.when(z < n_gy - 1)
+                    def _():
+                        copy.start()
 
             @pl.when(z + s <= n_gy - 1)
             def _():
                 copy = chain_copy(kind, c, 1, z + s)
                 copy.wait_recv()
-
-                @pl.when(z > 0)
-                def _():
-                    copy.start()
+                if s >= 2:
+                    @pl.when(z > 0)
+                    def _():
+                        copy.start()
 
     def drain(index):
         kind, c = chunks[index]
-        for s in range(n_gy):
+        for hops in (1, 2):
+            @pl.when(z + hops < n_gy)
+            def _():
+                chain_copy(kind, c, 0, z, hops).wait_send()
+
+            @pl.when(z - hops >= 0)
+            def _():
+                chain_copy(kind, c, 1, z, hops).wait_send()
+
+        for s in range(2, n_gy):
             @pl.when((z - s >= 0) & (z < n_gy - 1))
             def _():
                 chain_copy(kind, c, 0, z - s).wait_send()
@@ -191,20 +205,18 @@
         else:
             buf, weight, load, acc, width = hall, mv, loads_m, acc_c, h_width
         load[c].wait()
-        outs = acc.shape[1]
-        tile = min(512, outs // 2)
-        left = buf[:, :, c * width:(c + 1) * width].reshape(tokens, width)
+        outs = acc.shape[0]
+        tile = min(TILE, outs)
+        flip[:width, :] = buf[c].reshape(tokens, width).T
 
         @pl.loop(0, outs // tile)
         def _(i):
             at = pl.ds(pl.multiple_of(i * tile, tile), tile)
-            product = lax.dot_general(
-                left, weight[c, at, :], (((1,), (1,)), ((), ())), preferred_element_type=F32
-            )
+            product = jnp.dot(weight[c, at, :], flip[:width, :], preferred_element_type=F32)
             if c == 0:
-                acc[:, at] = product
+                acc[at, :] = product
             else:
-                acc[:, at] += product
+                acc[at, :] += product
 
     def to_partner(k, term, part, send, recv):
         return pltpu.make_async_remote_copy(
@@ -221,9 +233,14 @@
         )
 
     def scatter_first(acc, term, part, send, recv):
-        size = acc.shape[0] // n_gx
-        for b in range(n_gx):
-            term[b] = acc[b * size:(b + 1) * size, :].astype(BF16)
+        width = min(512, acc.shape[0] // 2)
+
+        @pl.loop(0, acc.shape[0] // width)
+        def _(i):
+            at = pl.ds(pl.multiple_of(i * width, width), width)
+            block = acc[at, :].astype(BF16).T
+            term[:, :, at] = block.reshape(n_gx, tokens // n_gx, width)
+
         for k in range(n_chips):
             to_partner(k, term, part, send, recv).start()
 
@@ -294,7 +311,7 @@
 
 
 def exchange(n_gx, n_gy, x, w, g, c, m, h):
-    g_chunks, h_chunks = 5, 4
+    g_chunks, h_chunks = (2 if g.shape[1] % 256 == 0 else 5), 4
     rows_g, rows_x = g.shape[0], x.shape[0]
     d, fp, ck, fm = x.shape[1], g.shape[1], c.shape[1], h.shape[1]
     tokens = rows_g * n_gy
@@ -316,21 +333,22 @@
         functools.partial(exchange_kernel, n_gx, n_gy, g_chunks, h_chunks),
         out_shape=(
             shape((d, tokens), BF16), shape((ck, tokens), BF16),
-            shape((n_gy, rows_g, fp), BF16), shape((n_gy, rows_g, fm), BF16),
+            shape((g_chunks, n_gy, rows_g, fp // g_chunks), BF16), shape((h_chunks, n_gy, rows_g, fm // h_chunks), BF16),
             shape((rows_x, d), BF16), shape((rows_x, ck), BF16),
         ),
         in_specs=[pl.BlockSpec(memory_space=ANY)] * 6,
         out_specs=[pl.BlockSpec(memory_space=ANY)] * 6,
         scratch_shapes=[
             vm((g_chunks, d, fp // g_chunks), BF16), vm((h_chunks, ck, fm // h_chunks), BF16),
-            vm((n_gy, rows_g, fp), BF16), vm((n_gy, rows_g, fm), BF16),
+            vm((g_chunks, n_gy, rows_g, fp // g_chunks), BF16), vm((h_chunks, n_gy, rows_g, fm // h_chunks), BF16),
             vm((n_gx, rows_x, d), BF16), vm((n_gx, rows_x, ck), BF16),
             vm((d, tokens), BF16), vm((ck, tokens), BF16),
-            vm((tokens, d), F32), vm((tokens, ck), F32),
+            vm((d, tokens), F32), vm((ck, tokens), F32),
+            vm((max(fp // g_chunks, fm // h_chunks), tokens), BF16),
             *scatter(d), *scatter(ck),
-            dma((g_chunks,)), dma((h_chunks,)), dma((4,)),
-            dma((2, n_gy, g_chunks)), dma((n_gy, g_chunks)),
-            dma((2, n_gy, h_chunks)), dma((n_gy, h_chunks)),
+            dma((g_chunks,)), dma((h_chunks,)), dma((2 + g_chunks + h_chunks,)),
+            dma((4, n_gy, g_chunks)), dma((n_gy, g_chunks)),
+            dma((4, n_gy, h_chunks)), dma((n_gy, h_chunks)),
             dma((2 * nc - 1,)), dma((2 * nc - 1,)), dma((2 * nc - 1,)), dma((2 * nc - 1,)),
             dma((nc,)), dma((nc,)), dma((more,)), dma((more,)),
             dma((nc,)), dma((nc,)), dma((more,)), dma((more,)),
@@ -347,19 +365,27 @@
 SLOTS = 3
 
 
-def gradients_kernel(g_steps, h_steps, xt, ct, gall, hall, dw, dm, xv, cv, gv, hv, wbuf, mbuf, in_sem, w_sem, m_sem):
+def gradients_kernel(
+    g_steps, h_steps, xt, ct, gall, hall, dx, dc, dw, dm, dx_out, dc_out,
+    xv, cv, gv, hv, dxv, dcv, wbuf, mbuf, in_sem, w_sem, m_sem,
+):
+    head = xt.shape[0] // g_steps
+    rest = pl.ds(head, xt.shape[0] - head)
     first = [
         pltpu.make_async_copy(gall, gv, in_sem.at[0]),
-        pltpu.make_async_copy(xt, xv, in_sem.at[1]),
+        pltpu.make_async_copy(xt.at[pl.ds(0, head), :], xv.at[pl.ds(0, head), :], in_sem.at[1]),
+        pltpu.make_async_copy(xt.at[rest, :], xv.at[rest, :], in_sem.at[4]),
         pltpu.make_async_copy(hall, hv, in_sem.at[2]),
         pltpu.make_async_copy(ct, cv, in_sem.at[3]),
+        pltpu.make_async_copy(dx, dxv, in_sem.at[5]),
+        pltpu.make_async_copy(dc, dcv, in_sem.at[6]),
     ]
     for copy in first:
         copy.start()
 
-    def run(steps, pieces, left, right, buf, sem, out):
+    def run(steps, left, right, buf, sem, out, late=None):
         tall = out.shape[0] // steps
-        wide = out.shape[1] // pieces
+        pieces, _, wide = right.shape
 
         def copy_out(i, slot):
             at = pl.ds(pl.multiple_of(i * tall, tall), tall)
@@ -372,12 +398,17 @@
             @pl.when(i >= SLOTS)
             def _():
                 copy_out(i - SLOTS, slot).wait()
+
+            if late is not None:
+                @pl.when(i == 1)
+                def _():
+                    late.wait()
 
             part = left[pl.ds(pl.multiple_of(i * tall, tall), tall), :]
             for p in range(pieces):
                 columns = slice(p * wide, (p + 1) * wide)
                 buf[slot, :, columns] = jnp.dot(
-                    part, right[:, columns], preferred_element_type=F32
+                    part, right[p], preferred_element_type=F32
                 ).astype(BF16)
             copy_out(i, slot).start()
 
@@ -385,38 +416,44 @@
 
     first[0].wait()
     first[1].wait()
-    last = run(g_steps, 5, xv, gv, wbuf, w_sem, dw)
-    first[2].wait()
-    first[3].wait()
-    last += run(h_steps, 4, cv, hv, mbuf, m_sem, dm)
-    for copy in last:
+    last = run(g_steps, xv, gv, wbuf, w_sem, dw, first[2])
+    for copy in first[3:]:
         copy.wait()
-
-
-def gradients(xt, ct, gall, hall):
+    small = [
+        pltpu.make_async_copy(dxv, dx_out, in_sem.at[5]),
+        pltpu.make_async_copy(dcv, dc_out, in_sem.at[6]),
+    ]
+    for copy in small:
+        copy.start()
+    last += run(h_steps, cv, hv, mbuf, m_sem, dm)
+    for copy in last + small:
+        copy.wait()
+
+
+def gradients(xt, ct, gall, hall, dx, dc):
     g_steps, h_steps = 8, 4
     d, tokens = xt.shape
     ck = ct.shape[0]
-    fp, fm = gall.shape[1], hall.shape[1]
+    fp, fm = gall.shape[0] * gall.shape[2], hall.shape[0] * hall.shape[2]
     dma = pltpu.SemaphoreType.DMA
     vm = pltpu.VMEM
     shape = jax.ShapeDtypeStruct
     return pl.pallas_call(
         functools.partial(gradients_kernel, g_steps, h_steps),
-        out_shape=(shape((d, fp), BF16), shape((ck, fm), BF16)),
-        in_specs=[pl.BlockSpec(memory_space=ANY)] * 4,
-        out_specs=[pl.BlockSpec(memory_space=ANY)] * 2,
+        out_shape=(shape((d, fp), BF16), shape((ck, fm), BF16), shape(dx.shape, BF16), shape(dc.shape, BF16)),
+        in_specs=[pl.BlockSpec(memory_space=ANY)] * 6,
+        out_specs=[pl.BlockSpec(memory_space=ANY)] * 4,
         scratch_shapes=[
-            vm((d, tokens), BF16), vm((ck, tokens), BF16), vm((tokens, fp), BF16), vm((tokens, fm), BF16),
+            vm((d, tokens), BF16), vm((ck, tokens), BF16), vm(gall.shape, BF16), vm(hall.shape, BF16), vm(dx.shape, BF16), vm(dc.shape, BF16),
             vm((SLOTS, d // g_steps, fp), BF16), vm((SLOTS, ck // h_steps, fm), BF16),
-            dma((4,)), dma((SLOTS,)), dma((SLOTS,)),
+            dma((7,)), dma((SLOTS,)), dma((SLOTS,)),
         ],
         compiler_params=pltpu.CompilerParams(vmem_limit_bytes=60 * 1024 * 1024),
         cost_estimate=pl.CostEstimate(
             flops=2 * tokens * (d * fp + ck * fm), bytes_accessed=2 * (d * fp + ck * fm), transcendentals=0
         ),
         name="gradients",
-    )(xt, ct, gall, hall)
+    )(xt, ct, gall, hall, dx, dc)
 
 
 def body(n_gx, n_gy, layer_input, packed_weight, packed_cotangent, context, mixing_weight, mixing_cotangent):
@@ -424,7 +461,9 @@
         n_gx, n_gy, layer_input, packed_weight, packed_cotangent, context, mixing_weight, mixing_cotangent
     )
     tokens = xt.shape[1]
-    dw, dm = gradients(xt, ct, gall.reshape(tokens, -1), hall.reshape(tokens, -1))
+    gall = gall.reshape(gall.shape[0], tokens, -1)
+    hall = hall.reshape(hall.shape[0], tokens, -1)
+    dw, dm, dx, dc = gradients(xt, ct, gall, hall, dx, dc)
     return dx, dw, dc, dm
 
 

time: 100 us -> 80 us (0.80)
  Pallas kernels: 97.9 us -> 79.1 us
  local copies, waits for them, and re-layouts: 1.43 us -> 0 us
    pallas_call x1, Pallas kernels: 82.1 us -> 63.9 us  [exchange(): pl.pallas_call(functools.partial(exchange_kernel, n_gx, n_gy, g_chunks, h...]
    unnamed x6 -> x0, local copies, waits for them, and re-layouts: 1.43 us -> none
where the time goes in v2:
time: 80 us; the launch traced here: 79.9 us
  Pallas kernels  79.1 us (99%)
  between operations  0.8 us (1%)
    pallas_call x1, Pallas kernels, exchange(): pl.pallas_call(functools.partial(exchange_kernel, n_gx, n_gy, g_chunks, h...  63.9 us
    pallas_call x1, Pallas kernels, gradients(): pl.pallas_call(functools.partial(gradients_kernel, g_steps, h_steps), out...  15.2 us

profile of v2, /device:TPU:0, one launch (start us, length us, event | category | flops | bytes accessed | tf_op | source)
XLA Modules:
  0.0 79.9 jit_solution(7595627292953271716)
XLA Ops:
  0.6 63.9 %exchange.1 = (bf16[4096,192]{1,0:T(8,128)(2,1)}, bf16[2048,192]{1,0:T(8,128)(2,1)}, bf16[2,4,48,1280]{3,2,1,0:T(8,128)(2,1)}, bf16[4,4,48,1024]{3,2,1,0:T(8,128...) custom-call(bf16[48,4096]{1,0:T(8,128)(2,1)} %x_in.1, bf16[4096,2560]{1,0:T(8,128)(2,1)} %w_in.1, ...), custom_call_target="tpu_custom_call" | custom-call | flops 7247757312 | bytes 37748736 | tf_op jit(solution)/shard_map/exchange/pallas_call | solution.py:332
  64.6 15.2 %gradients.1 = (bf16[4096,2560]{1,0:T(8,128)(2,1)}, bf16[2048,4096]{1,0:T(8,128)(2,1)}, bf16[48,4096]{1,0:T(8,128)(2,1)}, bf16[48,2048]{1,0:T(8,128)(2,1)}) custom-call(bf16[4096,192]{1,0:T(8,128)(2,1)} %get-tuple-element.14.xt, bf16[2048,192]{1,0:T(8,128)(2,1)} %get-tuple-element.15.ct, bf16[2,192,1280]{2,1,0:T(8,128)(2,1)} %bitcast.3, ...), custom_call_target="tpu_custom_call" | custom-call | flops 7247757312 | bytes 37748736 | tf_op jit(solution)/shard_map/gradients/pallas_call | solution.py:441
